TPU v7x, 256 devices: a whole 4x4x8 slice. The times are simulated.
256 devices in a mesh: row: 8 (over y, x_hi), col: 32 (over x_lo, z, core).
Axes of the slice: x: 4 (x_hi: 2, x_lo: 2; x = x_hi * 2 + x_lo), y: 4, z: 8, core: 2. Of those that a mesh axis runs over, the one named last changes fastest.
Arguments:
- inputs: bfloat16 [1024, 12288], P('col', 'row'), may hold values from -6 to 6
- out_grad: bfloat16 [1024, 12288], P('col', 'row'), may hold values from -6 to 6
- pre_act: bfloat16 [1024, 24576], P('row', 'col'), may hold values from -6 to 6
- w_up: bfloat16 [12288, 24576], P('row', 'col'), may hold values from -0.0546875 to 0.0546875
- w_down: bfloat16 [24576, 12288], P('col', 'row'), may hold values from -0.0390625 to 0.0390625
Outputs:
- input_grad: bfloat16 [1024, 12288], P('col', 'row')
- up_grad: bfloat16 [12288, 24576], P('row', 'col')
- down_grad: bfloat16 [24576, 12288], P('col', 'row')
All inputs are finite; a program needn't handle non-finite values.
Results may differ from a plain program's by a relative error of at most 0.0051.
Values may be sent and summed in bfloat16 or wider, within the bound.
A program may use at most 128 MiB of HBM per device.

v0:
```python
import jax
import jax.numpy as jnp
from jax import lax
from jax.sharding import PartitionSpec as P


def slope_and_act(pre):
    hval = pre.astype(jnp.float32)
    coeff = 0.7978845608028654
    inner = coeff * (hval + 0.044715 * hval * hval * hval)
    tanh_val = jnp.tanh(inner)
    slope = 0.5 * (1.0 + tanh_val) + 0.5 * hval * (1.0 - tanh_val * tanh_val) * coeff * (
        1.0 + 3.0 * 0.044715 * hval * hval
    )
    act = (0.5 * hval * (1.0 + tanh_val)).astype(jnp.bfloat16)
    return (slope, act)


def per_device(inputs, out_grad, pre_act, w_up, w_down):
    inputs_all, grads_all = (
        lax.all_gather(inputs, "col", axis=0, tiled=True),
        lax.all_gather(out_grad, "col", axis=0, tiled=True),
    )
    total_rows = grads_all.shape[0]
    scale = float(total_rows) ** (-0.5)
    part = grads_all
    act_grad = lax.psum_scatter(
        lax.dot_general(part, w_down, (((1,), (1,)), ((), ())), preferred_element_type=jnp.float32),
        "row",
        scatter_dimension=0,
        tiled=True,
    )
    slope, act_here = slope_and_act(pre_act)
    hidden_here = (act_grad * slope).astype(jnp.bfloat16)
    acts_all, hidden_all = (
        lax.all_gather(act_here, "row", axis=0, tiled=True),
        lax.all_gather(hidden_here, "row", axis=0, tiled=True),
    )
    up_part = lax.dot_general(
        inputs_all, hidden_all, (((0,), (0,)), ((), ())), preferred_element_type=jnp.float32
    )
    down_part = lax.dot_general(
        acts_all, grads_all, (((0,), (0,)), ((), ())), preferred_element_type=jnp.float32
    )
    up_grad = (up_part * scale).astype(jnp.bfloat16)
    down_grad = (down_part * scale).astype(jnp.bfloat16)
    part = hidden_all
    input_grad = lax.psum_scatter(
        lax.dot_general(part, w_up, (((1,), (1,)), ((), ())), preferred_element_type=jnp.float32),
        "col",
        scatter_dimension=0,
        tiled=True,
    )
    return (input_grad.astype(jnp.bfloat16), up_grad, down_grad)


def solution(mesh):
    return jax.shard_map(
        per_device,
        mesh=mesh,
        in_specs=(
            P("col", "row"),
            P("col", "row"),
            P("row", "col"),
            P("row", "col"),
            P("col", "row"),
        ),
        out_specs=(P("col", "row"), P("row", "col"), P("col", "row")),
        check_vma=False,
    )
```

profile of v0, /device:TPU:1, one launch (start us, length us, event | category | flops | bytes accessed | tf_op | source)
XLA Modules:
  0.0 482.3 jit_solution(11362313517838885214)
XLA Ops:
  7.2 0.0 copy-start
  7.2 0.0 all-gather.5.cloned.1.call-start
  7.2 0.7 all-gather.5.cloned.1.call-update
  7.9 0.0 reduce-scatter.3.cloned.1.call-start
  8.0 72.3 %all-gather.5.cloned.1.call-done = bf16[1024,1536]{1,0:T(8,128)(2,1)} async-done(((bf16[32,1536]{1,0:T(8,128)(2,1)}), bf16[1024,1536]{1,0:T(8,128)(2,1)}) %all-gather.5.cloned.1.call-update) | async-done | bytes 3145744 | tf_op jit(solution)/shard_map/all_gather | solution.py:22
  80.2 6.9 %fusion.12 = f32[1024,768]{1,0:T(8,128)} fusion(bf16[1024,1536]{1,0:T(8,128)(2,1)} %all-gather.5.cloned.1.call-done, bf16[768,1536]{1,0:T(8,128)(2,1)} %param.9), kind=kOutput, calls=%fused_computation.21 | convolution fusion | flops 2415919104 | bytes 8650752 | tf_op jit(solution)/shard_map/dot_general | solution.py:28
  87.1 0.0 copy-start.1
  87.1 0.0 reduce-scatter.3.cloned.1.call-update
  87.1 0.0 all-gather.7.cloned.1.call-start
  87.2 82.4 %reduce-scatter.3.cloned.1.call-done = f32[128,768]{1,0:T(8,128)} async-done(((f32[1024,768]{1,0:T(8,128)}), f32[128,768]{1,0:T(8,128)}) %reduce-scatter.3.cloned.1.call-update) | async-done | bytes 393232 | tf_op jit(solution)/shard_map/reduce_scatter | solution.py:27
  169.6 0.0 copy-done.1
  169.6 2.0 fusion.8
  171.6 0.0 all-gather.7.cloned.1.call-update
  171.7 0.0 all-gather.9.cloned.1.call-start
  171.7 0.5 all-gather.9.cloned.1.call-update
  172.3 0.0 all-gather.11.cloned.1.call-start
  172.3 0.5 all-gather.11.cloned.1.call-update
  172.8 0.0 reduce-scatter.5.cloned.1.call-start
  172.9 54.2 %all-gather.7.cloned.1.call-done = bf16[1024,768]{1,0:T(8,128)(2,1)} async-done(((bf16[128,768]{1,0:T(8,128)(2,1)}), bf16[1024,768]{1,0:T(8,128)(2,1)}) %all-gather.7.cloned.1.call-update) | async-done | bytes 1572880 | tf_op jit(solution)/shard_map/all_gather | solution.py:37
  227.1 0.0 copy-done
  227.1 6.1 %fusion.13 = f32[1024,1536]{1,0:T(8,128)} fusion(bf16[1024,768]{1,0:T(8,128)(2,1)} %all-gather.7.cloned.1.call-done, bf16[1536,768]{1,0:T(8,128)(2,1)S(1)} %copy-done), kind=kOutput, calls=%fused_computation.22 | convolution fusion | flops 2415919104 | bytes 10223616 | tf_op jit(solution)/shard_map/dot_general | solution.py:49
  233.2 0.0 reduce-scatter.5.cloned.1.call-update
  233.2 61.4 %all-gather.9.cloned.1.call-done = bf16[1024,1536]{1,0:T(8,128)(2,1)} async-done(((bf16[32,1536]{1,0:T(8,128)(2,1)}), bf16[1024,1536]{1,0:T(8,128)(2,1)}) %all-gather.9.cloned.1.call-update) | async-done | bytes 3145744 | tf_op jit(solution)/shard_map/all_gather | solution.py:21
  294.6 6.4 %fusion = bf16[1536,768]{0,1:T(8,128)(2,1)} fusion(bf16[1024,768]{1,0:T(8,128)(2,1)} %all-gather.7.cloned.1.call-done, bf16[1024,1536]{1,0:T(8,128)(2,1)} %all-gather.9.cloned.1.call-done), kind=kOutput, calls=%fused_computation.2 | convolution fusion | flops 2418278400 | bytes 7077888 | tf_op jit(solution)/shard_map/dot_general | solution.py:39
  301.0 4.3 copy.8
  305.3 45.1 %all-gather.11.cloned.1.call-done = bf16[1024,768]{1,0:T(8,128)(2,1)} async-done(((bf16[128,768]{1,0:T(8,128)(2,1)}), bf16[1024,768]{1,0:T(8,128)(2,1)}) %all-gather.11.cloned.1.call-update) | async-done | bytes 1572880 | tf_op jit(solution)/shard_map/all_gather | solution.py:36
  350.4 6.4 %multiply_convert_fusion = bf16[768,1536]{1,0:T(8,128)(2,1)} fusion(bf16[1024,768]{1,0:T(8,128)(2,1)} %all-gather.11.cloned.1.call-done, bf16[1024,1536]{1,0:T(8,128)(2,1)} %all-gather.5.cloned.1.call-done), kind=kOutput, calls=%fused_computation | convolution fusion | flops 2418278400 | bytes 7077888 | tf_op jit(solution)/shard_map/dot_general | solution.py:42
  356.8 117.0 %reduce-scatter.5.cloned.1.call-done = f32[32,1536]{1,0:T(8,128)} async-done(((f32[1024,1536]{1,0:T(8,128)}), f32[32,1536]{1,0:T(8,128)}) %reduce-scatter.5.cloned.1.call-update) | async-done | bytes 196624 | tf_op jit(solution)/shard_map/reduce_scatter | solution.py:48
  473.9 1.6 convert_element_type.23
Async XLA Ops:
  7.2 219.9 %copy-start = (bf16[1536,768]{1,0:T(8,128)(2,1)S(1)}, bf16[1536,768]{1,0:T(8,128)(2,1)}, u32[]{:S(2)}) copy-start(bf16[1536,768]{1,0:T(8,128)(2,1)} %param.8) | copy-start | bytes 7077892
  7.2 73.0 %all-gather.5.cloned.1.call-start = ((), (), s32[]{:S(2)}) async-start(), calls=%async_computation.2 | async-start | bytes 3244032 | tf_op jit(solution)/shard_map/all_gather | solution.py:22
  7.9 161.7 %reduce-scatter.3.cloned.1.call-start = ((), (), s32[]{:S(2)}) async-start(), calls=%async_computation.3 | async-start | bytes 3538944 | tf_op jit(solution)/shard_map/reduce_scatter | solution.py:27
  87.1 82.5 %copy-start.1 = (bf16[128,768]{1,0:T(8,128)(2,1)S(1)}, bf16[128,768]{1,0:T(8,128)(2,1)}, u32[]{:S(2)}) copy-start(bf16[128,768]{1,0:T(8,128)(2,1)} %param.7) | copy-start | bytes 589828
  87.1 139.9 %all-gather.7.cloned.1.call-start = ((), (), s32[]{:S(2)}) async-start(), calls=%async_computation.4 | async-start | bytes 1769472 | tf_op jit(solution)/shard_map/all_gather | solution.py:37
  171.7 122.9 %all-gather.9.cloned.1.call-start = ((), (), s32[]{:S(2)}) async-start(), calls=%async_computation.6 | async-start | bytes 3244032 | tf_op jit(solution)/shard_map/all_gather | solution.py:21
  172.3 178.2 %all-gather.11.cloned.1.call-start = ((), (), s32[]{:S(2)}) async-start(), calls=%async_computation.7 | async-start | bytes 1769472 | tf_op jit(solution)/shard_map/all_gather | solution.py:36
  172.8 301.0 %reduce-scatter.5.cloned.1.call-start = ((), (), s32[]{:S(2)}) async-start(), calls=%async_computation.5 | async-start | bytes 6488064 | tf_op jit(solution)/shard_map/reduce_scatter | solution.py:48
Sparse Core Ops, SparseCore 0:
  9.9 70.2 all-gather.4
  87.3 82.3 reduce-scatter.2
  172.8 54.2 all-gather.6
  228.8 65.7 all-gather.8
  297.0 53.3 all-gather.10
  352.8 120.9 reduce-scatter.4
where the time goes:
time: 485 us; the launch traced here: 482 us
  waiting for transfers between devices  434 us (89%)
  matrix products  25.8 us (5%)
  between operations  14.1 us (3%)
    reduce_scatter x1, waiting for transfers between devices, per_device(): lax.psum_scatter(lax.dot_general(part, w_up, (((1,), (1,)), ((), ())), pr...  117 us
    reduce_scatter x1, waiting for transfers between devices, per_device(): lax.psum_scatter(lax.dot_general(part, w_down, (((1,), (1,)), ((), ())),...  82.4 us
    all_gather x1, waiting for transfers between devices, per_device(): lax.all_gather(out_grad, 'col', axis=0, tiled=True)  72.3 us
    all_gather x1, waiting for transfers between devices, per_device(): lax.all_gather(inputs, 'col', axis=0, tiled=True)  61.4 us
    all_gather x1, waiting for transfers between devices, per_device(): lax.all_gather(hidden_here, 'row', axis=0, tiled=True)  54.2 us
    all_gather x1, waiting for transfers between devices, per_device(): lax.all_gather(act_here, 'row', axis=0, tiled=True)  45.1 us
  transfers between devices with their start and end apart: 6, of which 6 were waited for; matrix products, arithmetic and copies ran while one was open for 5% of the time, Pallas kernels for 0%

commit v1 on v0

v1 whole, which is shorter than its diff:
```python
import functools

import jax
import jax.numpy as jnp
from jax import lax
from jax.experimental import pallas as pl
from jax.experimental.pallas import tpu as pltpu
from jax.sharding import PartitionSpec as P

MESH = pl.DeviceIdType.MESH
BF16 = jnp.bfloat16
F32 = jnp.float32
NT = (((1,), (1,)), ((), ()))
TN = (((0,), (0,)), ((), ()))
COLS = 16
ROWS = 8
TILE = 256


def kernel(
    H,
    in_ref, og_ref, pre_ref, wup_hbm, wdn_hbm,
    ig_out, up_hbm, dn_hbm,
    wup, wdn, slope, grads, ins, acts, part, rsr, hid, igs, igr, igf, igb, fin, up, dn,
    wsem, gs, gr, gfs, gfr, xs, xr, xfs, xfr, as_, ar, ps, pr, hs, hr, ss, sr, is_, ir, osem,
):
    R = 32 // H
    D = in_ref.shape[1]
    F = pre_ref.shape[1]
    row = lax.axis_index("row")
    col = lax.axis_index("col")
    chip = lax.div(col, 2)
    k = lax.rem(col, 2)
    y, xh = lax.div(row, 2), lax.rem(row, 2)
    xl, z = lax.div(chip, 8), lax.rem(chip, 8)

    def chip_at(o):
        return lax.rem(xl + lax.div(o, 8), 2) * 8 + lax.rem(z + o, 8)

    def col_dev(o):
        return (row, chip_at(o) * 2 + k)

    def row_at(o):
        return lax.rem(y + o, 4) * 2 + lax.rem(xh + lax.div(o, 4), 2)

    def row_dev(o):
        return (row_at(o), col)

    sib = (row, chip * 2 + 1 - k)

    def each(lo, hi, f):
        def body(o, carry):
            f(o)
            return carry
        lax.fori_loop(lo, hi, body, 0)

    def remote(src, dst, send, recv, dev):
        return pltpu.make_async_remote_copy(
            src_ref=src, dst_ref=dst, send_sem=send, recv_sem=recv, device_id=dev, device_id_type=MESH
        )

    wdn_copy = pltpu.make_async_copy(wdn_hbm, wdn, wsem.at[0])
    wup_copy = pltpu.make_async_copy(wup_hbm, wup, wsem.at[1])
    wdn_copy.start()
    wup_copy.start()

    barrier = pltpu.get_barrier_semaphore()
    each(1, COLS, lambda o: pl.semaphore_signal(barrier, inc=1, device_id=col_dev(o), device_id_type=MESH))
    each(1, ROWS, lambda o: pl.semaphore_signal(barrier, inc=1, device_id=row_dev(o), device_id_type=MESH))
    pl.semaphore_signal(barrier, inc=1, device_id=sib, device_id_type=MESH)
    pl.semaphore_wait(barrier, COLS + ROWS - 1)

    def c_grad(h, o):
        return remote(og_ref.at[pl.ds(h * R, R)], grads.at[chip, k, h], gs.at[h, o], gr.at[h, o], col_dev(o))

    def c_gradf(h):
        return remote(grads.at[:, k, h], grads.at[:, k, h], gfs.at[h], gfr.at[h], sib)

    def c_in(o):
        return remote(in_ref, ins.at[chip, k], xs.at[o], xr.at[o], col_dev(o))

    def c_inf():
        return remote(ins.at[:, k], ins.at[:, k], xfs, xfr, sib)

    def c_act(o):
        return remote(acts.at[pl.ds(2 * row, 2)], acts.at[pl.ds(2 * row, 2)], as_.at[o], ar.at[o], row_dev(o))

    def c_part(h, q, o):
        kk = k if q == 0 else 1 - k
        return remote(
            part.at[pl.ds(2 * row_at(o), 2), kk, h], rsr.at[o, :, kk, h], ps.at[h, q, o], pr.at[h, q, o], row_dev(o)
        )

    def c_hid(h, o):
        block = hid.at[pl.ds(2 * row, 2), :, h]
        return remote(block, block, hs.at[h, o], hr.at[h, o], row_dev(o))

    def c_igs(h):
        return remote(igs.at[h], igr.at[h], ss.at[h], sr.at[h], sib)

    def c_ig(h, o):
        return remote(igb.at[h, chip_at(o)], fin.at[o, h], is_.at[h, o], ir.at[h, o], col_dev(o))

    for h in range(H):
        each(1, COLS, lambda o: c_grad(h, o).start())
        grads[chip, k, h] = og_ref[h * R:(h + 1) * R]
    ins[chip, k] = in_ref[...]

    def gelu(b):
        hval = pre_ref[pl.ds(b * 32, 32), :].astype(F32)
        coeff = 0.7978845608028654
        inner = coeff * (hval + 0.044715 * hval * hval * hval)
        t = jnp.tanh(inner)
        act = (0.5 * hval * (1.0 + t)).astype(BF16)
        acts[2 * row + lax.div(b, 2), lax.rem(b, 2)] = act
        sl = 0.5 * (1.0 + t) + 0.5 * hval * (1.0 - t * t) * coeff * (1.0 + 3.0 * 0.044715 * hval * hval)
        for h in range(H):
            slope[lax.div(b, 2), lax.rem(b, 2), h] = sl[h * R:(h + 1) * R]

    each(0, 4, gelu)
    each(1, ROWS, lambda o: c_act(o).start())

    def mm1(h, kk):
        def tile(n):
            cols = pl.ds(pl.multiple_of(n * TILE, TILE), TILE)
            lhs = grads[:, kk, h].reshape(16 * R, D)
            acc = lax.dot_general(lhs, wdn[cols, :], NT, preferred_element_type=F32)
            part[:, kk, h, :, cols] = acc.astype(BF16).reshape(16, R, TILE)
        each(0, F // TILE, tile)

    wdn_copy.wait()
    for h in range(H):
        each(1, COLS, lambda o: c_grad(h, o).wait_recv())
        c_gradf(h).start()
        mm1(h, k)
        each(1, ROWS, lambda o: c_part(h, 0, o).start())
        c_gradf(h).wait_recv()
        mm1(h, 1 - k)
        each(1, ROWS, lambda o: c_part(h, 1, o).start())

    each(1, COLS, lambda o: c_in(o).start())

    scale = 0.03125

    def c_dn(m):
        rows = pl.ds(m * TILE, TILE)
        return pltpu.make_async_copy(dn.at[rows], dn_hbm.at[rows], osem.at[m])

    def mm_dn(m):
        cols = pl.ds(pl.multiple_of(m * TILE, TILE), TILE)
        lhs = acts[:, :, :, cols].reshape(1024, TILE)
        def half(n):
            oc = pl.ds(pl.multiple_of(n * 512, 512), 512)
            rhs = grads[:, :, :, :, oc].reshape(1024, 512)
            acc = lax.dot_general(lhs, rhs, TN, preferred_element_type=F32)
            dn[pl.ds(m * TILE, TILE), oc] = (acc * scale).astype(BF16)
        each(0, D // 512, half)
        c_dn(m).start()

    def hidden(h):
        each(1, ROWS, lambda o: c_part(h, 0, o).wait_recv())
        each(1, ROWS, lambda o: c_part(h, 1, o).wait_recv())

        def block(b):
            zz, kk = lax.div(b, 2), lax.rem(b, 2)
            acc = part[2 * row + zz, kk, h].astype(F32)
            for o in range(1, ROWS):
                acc += rsr[o, zz, kk, h].astype(F32)
            hid[2 * row + zz, kk, h] = (acc * slope[zz, kk, h]).astype(BF16)

        each(0, 4, block)
        each(1, ROWS, lambda o: c_hid(h, o).start())

    for h in range(H):
        hidden(h)

    each(1, ROWS, lambda o: c_act(o).wait_recv())
    each(0, F // TILE, mm_dn)

    def mm_ig(h, kk, put):
        def tile(n):
            cols = pl.ds(pl.multiple_of(n * TILE, TILE), TILE)
            lhs = hid[:, kk, h].reshape(16 * R, F)
            acc = lax.dot_general(lhs, wup[cols, :], NT, preferred_element_type=F32)
            put(cols, acc.reshape(16, R, TILE))
        each(0, D // TILE, tile)

    def put_sib(h):
        def put(cols, acc):
            igs[h, :, :, cols] = acc.astype(BF16)
        return put

    def put_own(cols, acc):
        igf[:, :, cols] = acc

    wup_copy.wait()
    for h in range(H):
        each(1, ROWS, lambda o: c_hid(h, o).wait_recv())
        mm_ig(h, 1 - k, put_sib(h))
        c_igs(h).start()
        mm_ig(h, k, put_own)
        c_igs(h).wait_recv()

        def add(j):
            igb[h, j] = (igf[j] + igr[h, j].astype(F32)).astype(BF16)

        each(0, COLS, add)
        each(1, COLS, lambda o: c_ig(h, o).start())

    each(1, COLS, lambda o: c_in(o).wait_recv())
    c_inf().start()
    c_inf().wait_recv()

    def c_up(m):
        rows = pl.ds(m * TILE, TILE)
        return pltpu.make_async_copy(up.at[rows], up_hbm.at[rows], osem.at[F // TILE + m])

    def mm_up(m):
        cols = pl.ds(pl.multiple_of(m * TILE, TILE), TILE)
        lhs = ins[:, :, :, cols].reshape(1024, TILE)
        rhs = hid[...].reshape(1024, F)
        acc = lax.dot_general(lhs, rhs, TN, preferred_element_type=F32)
        up[pl.ds(m * TILE, TILE), :] = (acc * scale).astype(BF16)
        c_up(m).start()

    each(0, D // TILE, mm_up)

    for h in range(H):
        each(1, COLS, lambda o: c_ig(h, o).wait_recv())

        def total(n):
            cols = pl.ds(pl.multiple_of(n * 512, 512), 512)
            acc = igb[h, chip, :, cols].astype(F32)
            for o in range(1, COLS):
                acc += fin[o, h, :, cols].astype(F32)
            ig_out[pl.ds(h * R, R), cols] = acc.astype(BF16)

        each(0, D // 512, total)

    for h in range(H):
        each(1, COLS, lambda o: c_grad(h, o).wait_send())
        c_gradf(h).wait_send()
        for q in range(2):
            each(1, ROWS, lambda o: c_part(h, q, o).wait_send())
        each(1, ROWS, lambda o: c_hid(h, o).wait_send())
        c_igs(h).wait_send()
        each(1, COLS, lambda o: c_ig(h, o).wait_send())
    each(1, COLS, lambda o: c_in(o).wait_send())
    c_inf().wait_send()
    each(1, ROWS, lambda o: c_act(o).wait_send())
    each(0, F // TILE, lambda m: c_dn(m).wait())
    each(0, D // TILE, lambda m: c_up(m).wait())


def per_device(H, inputs, out_grad, pre_act, w_up, w_down):
    R = 32 // H
    D = inputs.shape[1]
    F = pre_act.shape[1]
    vmem = pl.BlockSpec(memory_space=pltpu.VMEM)
    hbm = pl.BlockSpec(memory_space=pl.ANY)
    dma = pltpu.SemaphoreType.DMA
    return pl.pallas_call(
        functools.partial(kernel, H),
        out_shape=(
            jax.ShapeDtypeStruct((32, D), BF16),
            jax.ShapeDtypeStruct((D, F), BF16),
            jax.ShapeDtypeStruct((F, D), BF16),
        ),
        in_specs=[vmem, vmem, vmem, hbm, hbm],
        out_specs=(vmem, hbm, hbm),
        scratch_shapes=[
            pltpu.VMEM((D, F), BF16),
            pltpu.VMEM((F, D), BF16),
            pltpu.VMEM((2, 2, H, R, F), F32),
            pltpu.VMEM((COLS, 2, H, R, D), BF16),
            pltpu.VMEM((COLS, 2, 32, D), BF16),
            pltpu.VMEM((COLS, 2, 32, F), BF16),
            pltpu.VMEM((COLS, 2, H, R, F), BF16),
            pltpu.VMEM((ROWS, 2, 2, H, R, F), BF16),
            pltpu.VMEM((COLS, 2, H, R, F), BF16),
            pltpu.VMEM((H, COLS, R, D), BF16),
            pltpu.VMEM((H, COLS, R, D), BF16),
            pltpu.VMEM((COLS, R, D), F32),
            pltpu.VMEM((H, COLS, R, D), BF16),
            pltpu.VMEM((COLS, H, R, D), BF16),
            pltpu.VMEM((D, F), BF16),
            pltpu.VMEM((F, D), BF16),
            dma((2,)),
            dma((H, COLS)), dma((H, COLS)), dma((H,)), dma((H,)),
            dma((COLS,)), dma((COLS,)), dma, dma,
            dma((ROWS,)), dma((ROWS,)),
            dma((H, 2, ROWS)), dma((H, 2, ROWS)),
            dma((H, ROWS)), dma((H, ROWS)),
            dma((H,)), dma((H,)),
            dma((H, COLS)), dma((H, COLS)),
            dma((F // TILE + D // TILE,)),
        ],
        compiler_params=pltpu.CompilerParams(
            collective_id=0, has_side_effects=True, vmem_limit_bytes=56 * 2**20
        ),
        cost_estimate=pl.CostEstimate(flops=8 * 1024 * 1536 * 768, bytes_accessed=10 * 2**20, transcendentals=128 * 768),
    )(inputs, out_grad, pre_act, w_up, w_down)


def solution(mesh):
    return jax.shard_map(
        functools.partial(per_device, 2),
        mesh=mesh,
        in_specs=(P("col", "row"), P("col", "row"), P("row", "col"), P("row", "col"), P("col", "row")),
        out_specs=(P("col", "row"), P("row", "col"), P("col", "row")),
        check_vma=False,
    )
```

time: 485 us -> 143 us (0.29)
  waiting for transfers between devices: 434 us -> 0 us
  Pallas kernels: 0 us -> 134 us
  matrix products: 25.8 us -> 0 us
  between operations: 14.1 us -> 0.64 us
    all_gather x4 -> x0, waiting for transfers between devices: 233 us -> none  [the longest x1 72.3 us: per_device(): lax.all_gather(out_grad, 'col', axis=0, tiled=True)]
    reduce_scatter x2 -> x0, waiting for transfers between devices: 199 us -> none  [the longest x1 117 us: per_device(): lax.psum_scatter(lax.dot_general(part, w_up, (((1,), (1,)), ((), ())), pr...]
    pallas_call x0 -> x1, Pallas kernels: none -> 134 us  [per_device(): pl.pallas_call(functools.partial(kernel, H), out_shape=(jax.ShapeDtypeStr...]
    dot_general x4 -> x0, matrix products: 25.8 us -> none  [the longest x1 6.89 us: per_device(): lax.dot_general(part, w_down, (((1,), (1,)), ((), ())), preferred_element...]
  transfers between devices with their start and end apart: 6 -> 0, of which waited for: 6 -> 0; matrix products, arithmetic and copies ran while one was open for 5% -> 0% of each run, Pallas kernels for 0% -> 0%
where the time goes in v1:
time: 143 us; the launch traced here: 141 us
  Pallas kernels  134 us (94%)
  local copies, waits for them, and re-layouts  6.32 us (4%)
    pallas_call x1, Pallas kernels, per_device(): pl.pallas_call(functools.partial(kernel, H), out_shape=(jax.ShapeDtypeStr...  134 us
    unnamed x5, local copies, waits for them, and re-layouts  6.32 us

profile of v1, /device:TPU:1, one launch (start us, length us, event | category | flops | bytes accessed | tf_op | source)
XLA Modules:
  0.0 141.1 jit_solution(6012654422618704399)
XLA Ops:
  0.6 134.1 %shard_map.76 = (bf16[32,1536]{1,0:T(8,128)(2,1)}, bf16[1536,768]{1,0:T(8,128)(2,1)}, bf16[768,1536]{1,0:T(8,128)(2,1)}) custom-call(bf16[32,1536]{1,0:T(8,128)(2,1)} %in_ref.1, bf16[32,1536]{1,0:T(8,128)(2,1)} %og_ref.1, bf16[128,768]{1,0:T(8,128)(2,1)} %pre_ref.1, bf16[1536,768]{1,0:T(8,128)(2,1)} %wup_hbm.1, bf16[768,1536]{1,0:T(8,128)(2,1)} %wdn_hbm.1), custom_call_target="tpu_custom_call" | custom-call | flops 9663676416 | bytes 10485760 | tf_op jit(solution)/shard_map/pallas_call | solution.py:262
  134.8 1.5 %copy.11 = bf16[32,1536]{1,0:T(8,128)(2,1)} copy(bf16[32,1536]{1,0:T(8,128)(2,1)} %get-tuple-element.6) | data formatting | bytes 196608
  136.3 0.0 copy-start
  136.3 3.4 %copy.12 = bf16[1536,768]{1,0:T(8,128)(2,1)} copy(bf16[1536,768]{1,0:T(8,128)(2,1)} %get-tuple-element.7) | data formatting | bytes 4718592
  139.7 0.0 copy-done
  139.7 1.4 copy.13
Async XLA Ops:
  136.3 3.4 %copy-start = (bf16[768,1536]{1,0:T(8,128)(2,1)S(1)}, bf16[768,1536]{1,0:T(8,128)(2,1)}, u32[]{:S(2)}) copy-start(bf16[768,1536]{1,0:T(8,128)(2,1)} %get-tuple-element.8) | copy-start | bytes 7077892

commit v2 on v1

--- a/solution.py
+++ b/solution.py
@@ -21,8 +21,9 @@
     H,
     in_ref, og_ref, pre_ref, wup_hbm, wdn_hbm,
     ig_out, up_hbm, dn_hbm,
-    wup, wdn, slope, grads, ins, acts, part, rsr, hid, igs, igr, igf, igb, fin, up, dn,
-    wsem, gs, gr, gfs, gfr, xs, xr, xfs, xfr, as_, ar, ps, pr, hs, hr, ss, sr, is_, ir, osem,
+    wup, wdn, slope, grads, ins, acts, part, rsr, hid, igs, igr, igf, igb, igx, igz, igo, fin, up, dn,
+    wsem, gxs, gxr, gs, gr, gfs, gfr, xxs, xxr, xs, xr, xfs, xfr, as_, ar, ps, pr, hs, hr, ss, sr,
+    bxs, bxr, is_, ir, osem,
 ):
     R = 32 // H
     D = in_ref.shape[1]
@@ -34,11 +35,14 @@
     y, xh = lax.div(row, 2), lax.rem(row, 2)
     xl, z = lax.div(chip, 8), lax.rem(chip, 8)
 
-    def chip_at(o):
-        return lax.rem(xl + lax.div(o, 8), 2) * 8 + lax.rem(z + o, 8)
-
-    def col_dev(o):
-        return (row, chip_at(o) * 2 + k)
+    def z_at(dz):
+        return lax.rem(z + dz, 8)
+
+    def z_dev(dz):
+        return (row, (xl * 8 + z_at(dz)) * 2 + k)
+
+    other = (1 - xl) * 8
+    partner = (row, (other + z) * 2 + k)
 
     def row_at(o):
         return lax.rem(y + o, 4) * 2 + lax.rem(xh + lax.div(o, 4), 2)
@@ -65,19 +69,36 @@
     wup_copy.start()
 
     barrier = pltpu.get_barrier_semaphore()
-    each(1, COLS, lambda o: pl.semaphore_signal(barrier, inc=1, device_id=col_dev(o), device_id_type=MESH))
+    each(1, 8, lambda o: pl.semaphore_signal(barrier, inc=1, device_id=z_dev(o), device_id_type=MESH))
+    pl.semaphore_signal(barrier, inc=1, device_id=partner, device_id_type=MESH)
     each(1, ROWS, lambda o: pl.semaphore_signal(barrier, inc=1, device_id=row_dev(o), device_id_type=MESH))
     pl.semaphore_signal(barrier, inc=1, device_id=sib, device_id_type=MESH)
-    pl.semaphore_wait(barrier, COLS + ROWS - 1)
-
-    def c_grad(h, o):
-        return remote(og_ref.at[pl.ds(h * R, R)], grads.at[chip, k, h], gs.at[h, o], gr.at[h, o], col_dev(o))
+    pl.semaphore_wait(barrier, 7 + 1 + 1 + ROWS - 1)
+
+    def ring_block(p, d, s):
+        return (xl * 8 if p == 0 else other) + z_at((9 - s) % 8 if d == 0 else s - 1)
+
+    def ring_ok(p, d, s):
+        return s < 4 or (s == 4 and p == d)
+
+    def c_gradx(h):
+        return remote(grads.at[chip, k, h], grads.at[chip, k, h], gxs.at[h], gxr.at[h], partner)
+
+    def c_grad(h, p, d, s):
+        block = grads.at[ring_block(p, d, s), k, h]
+        i = (p * 2 + d) * 4 + s - 1
+        return remote(block, block, gs.at[h, i], gr.at[h, i], z_dev(1 if d == 0 else 7))
+
+    def c_inx():
+        return remote(ins.at[chip, k], ins.at[chip, k], xxs, xxr, partner)
+
+    def c_in(p, d, s):
+        block = ins.at[ring_block(p, d, s), k]
+        i = (p * 2 + d) * 4 + s - 1
+        return remote(block, block, xs.at[i], xr.at[i], z_dev(1 if d == 0 else 7))
 
     def c_gradf(h):
         return remote(grads.at[:, k, h], grads.at[:, k, h], gfs.at[h], gfr.at[h], sib)
-
-    def c_in(o):
-        return remote(in_ref, ins.at[chip, k], xs.at[o], xr.at[o], col_dev(o))
 
     def c_inf():
         return remote(ins.at[:, k], ins.at[:, k], xfs, xfr, sib)
@@ -95,15 +116,20 @@
         block = hid.at[pl.ds(2 * row, 2), :, h]
         return remote(block, block, hs.at[h, o], hr.at[h, o], row_dev(o))
 
-    def c_igs(h):
-        return remote(igs.at[h], igr.at[h], ss.at[h], sr.at[h], sib)
+    def c_igs(h, c):
+        return remote(igs.at[h, c, :, 1 - k], igr.at[h, c], ss.at[h, c], sr.at[h, c], sib)
+
+    def c_igx(h, o):
+        return remote(igb.at[h, z_at(o)], igx.at[h, z_at(o)], bxs.at[h, o], bxr.at[h, o], partner)
 
     def c_ig(h, o):
-        return remote(igb.at[h, chip_at(o)], fin.at[o, h], is_.at[h, o], ir.at[h, o], col_dev(o))
+        return remote(igz.at[h, z_at(o)], fin.at[o, h], is_.at[h, o], ir.at[h, o], z_dev(o))
 
     for h in range(H):
-        each(1, COLS, lambda o: c_grad(h, o).start())
         grads[chip, k, h] = og_ref[h * R:(h + 1) * R]
+        for d in range(2):
+            c_grad(h, 0, d, 1).start()
+        c_gradx(h).start()
     ins[chip, k] = in_ref[...]
 
     def gelu(b):
@@ -128,17 +154,44 @@
             part[:, kk, h, :, cols] = acc.astype(BF16).reshape(16, R, TILE)
         each(0, F // TILE, tile)
 
-    wdn_copy.wait()
     for h in range(H):
-        each(1, COLS, lambda o: c_grad(h, o).wait_recv())
+        c_gradx(h).wait_recv()
+        for d in range(2):
+            c_grad(h, 1, d, 1).start()
+    def grad_step(h, s):
+        for p in range(2):
+            for d in range(2):
+                if ring_ok(p, d, s):
+                    c_grad(h, p, d, s).wait_recv()
+                    if ring_ok(p, d, s + 1):
+                        c_grad(h, p, d, s + 1).start()
+
+    for s in range(1, 4):
+        for h in range(H):
+            grad_step(h, s)
+
+    for h in range(H):
+        grad_step(h, 4)
         c_gradf(h).start()
+        if h == H - 1:
+            c_inx().start()
+            for d in range(2):
+                c_in(0, d, 1).start()
+        if h == 0:
+            wdn_copy.wait()
         mm1(h, k)
         each(1, ROWS, lambda o: c_part(h, 0, o).start())
         c_gradf(h).wait_recv()
         mm1(h, 1 - k)
         each(1, ROWS, lambda o: c_part(h, 1, o).start())
 
-    each(1, COLS, lambda o: c_in(o).start())
+    def in_step(s):
+        for p in range(2):
+            for d in range(2):
+                if ring_ok(p, d, s):
+                    c_in(p, d, s).wait_recv()
+                    if ring_ok(p, d, s + 1):
+                        c_in(p, d, s + 1).start()
 
     scale = 0.03125
 
@@ -171,44 +224,82 @@
         each(0, 4, block)
         each(1, ROWS, lambda o: c_hid(h, o).start())
 
-    for h in range(H):
-        hidden(h)
-
     each(1, ROWS, lambda o: c_act(o).wait_recv())
-    each(0, F // TILE, mm_dn)
-
-    def mm_ig(h, kk, put):
+    c_inx().wait_recv()
+    for d in range(2):
+        c_in(1, d, 1).start()
+    if H == 1:
+        in_step(1)
+        mm_dn(0)
+        hidden(0)
+        in_step(2)
+        mm_dn(1)
+        in_step(3)
+        mm_dn(2)
+        in_step(4)
+    else:
+        in_step(1)
+        hidden(0)
+        mm_dn(0)
+        in_step(2)
+        hidden(1)
+        mm_dn(1)
+        in_step(3)
+        mm_dn(2)
+
+    def mm_ig(h, c):
+        first = other if c == 0 else xl * 8
         def tile(n):
             cols = pl.ds(pl.multiple_of(n * TILE, TILE), TILE)
-            lhs = hid[:, kk, h].reshape(16 * R, F)
-            acc = lax.dot_general(lhs, wup[cols, :], NT, preferred_element_type=F32)
-            put(cols, acc.reshape(16, R, TILE))
+            lhs = hid[pl.ds(first, 8), :, h].reshape(16 * R, F)
+            acc = lax.dot_general(lhs, wup[cols, :], NT, preferred_element_type=F32).reshape(8, 2, R, TILE)
+            igf[h, c, :, :, :, cols] = acc
+            igs[h, c, :, :, :, cols] = acc.astype(BF16)
         each(0, D // TILE, tile)
 
-    def put_sib(h):
-        def put(cols, acc):
-            igs[h, :, :, cols] = acc.astype(BF16)
-        return put
-
-    def put_own(cols, acc):
-        igf[:, :, cols] = acc
+    def share(h, o):
+        j = z_at(o)
+        igb[h, j] = (igf[h, 0, j, k] + igr[h, 0, j].astype(F32)).astype(BF16)
+        c_igx(h, o).start()
+
+    def pass_on(h, o):
+        j = z_at(o)
+        c_igx(h, o).wait_recv()
+        acc = igf[h, 1, j, k] + igr[h, 1, j].astype(F32) + igx[h, j].astype(F32)
+        if o == 0:
+            igo[h] = acc
+        else:
+            igz[h, j] = acc.astype(BF16)
+            c_ig(h, o).start()
+
+    order = (4, 3, 5, 2, 6, 1, 7, 0)
+
+    def ig(h):
+        each(1, ROWS, lambda o: c_hid(h, o).wait_recv())
+        mm_ig(h, 0)
+        c_igs(h, 0).start()
+        mm_ig(h, 1)
+        c_igs(h, 1).start()
+        c_igs(h, 0).wait_recv()
+        for o in order:
+            share(h, o)
+        if h == 0:
+            if H == 2:
+                in_step(4)
+            c_inf().start()
+        c_igs(h, 1).wait_recv()
 
     wup_copy.wait()
-    for h in range(H):
-        each(1, ROWS, lambda o: c_hid(h, o).wait_recv())
-        mm_ig(h, 1 - k, put_sib(h))
-        c_igs(h).start()
-        mm_ig(h, k, put_own)
-        c_igs(h).wait_recv()
-
-        def add(j):
-            igb[h, j] = (igf[j] + igr[h, j].astype(F32)).astype(BF16)
-
-        each(0, COLS, add)
-        each(1, COLS, lambda o: c_ig(h, o).start())
-
-    each(1, COLS, lambda o: c_in(o).wait_recv())
-    c_inf().start()
+    ig(0)
+    if H == 2:
+        for o in order[:4]:
+            pass_on(0, o)
+        ig(1)
+        for o in order[4:]:
+            pass_on(0, o)
+    for o in order:
+        pass_on(H - 1, o)
+
     c_inf().wait_recv()
 
     def c_up(m):
@@ -226,30 +317,55 @@
     each(0, D // TILE, mm_up)
 
     for h in range(H):
-        each(1, COLS, lambda o: c_ig(h, o).wait_recv())
+        each(1, 8, lambda o: c_ig(h, o).wait_recv())
 
         def total(n):
             cols = pl.ds(pl.multiple_of(n * 512, 512), 512)
-            acc = igb[h, chip, :, cols].astype(F32)
-            for o in range(1, COLS):
+            acc = igo[h, :, cols]
+            for o in range(1, 8):
                 acc += fin[o, h, :, cols].astype(F32)
             ig_out[pl.ds(h * R, R), cols] = acc.astype(BF16)
 
         each(0, D // 512, total)
 
+    for p in range(2):
+        for d in range(2):
+            for t in range(1, 5):
+                if ring_ok(p, d, t):
+                    for h in range(H):
+                        c_grad(h, p, d, t).wait_send()
+                    c_in(p, d, t).wait_send()
     for h in range(H):
-        each(1, COLS, lambda o: c_grad(h, o).wait_send())
+        c_gradx(h).wait_send()
         c_gradf(h).wait_send()
         for q in range(2):
             each(1, ROWS, lambda o: c_part(h, q, o).wait_send())
         each(1, ROWS, lambda o: c_hid(h, o).wait_send())
-        c_igs(h).wait_send()
-        each(1, COLS, lambda o: c_ig(h, o).wait_send())
-    each(1, COLS, lambda o: c_in(o).wait_send())
+        for c in range(2):
+            c_igs(h, c).wait_send()
+        each(0, 8, lambda o: c_igx(h, o).wait_send())
+        each(1, 8, lambda o: c_ig(h, o).wait_send())
+    c_inx().wait_send()
     c_inf().wait_send()
     each(1, ROWS, lambda o: c_act(o).wait_send())
     each(0, F // TILE, lambda m: c_dn(m).wait())
     each(0, D // TILE, lambda m: c_up(m).wait())
+
+
+def copy_kernel(ig, up, dn, ig_out, up_out, dn_out, ig_v, up_v, dn_v, sem):
+    steps = [(ig, ig_v, ig_out, pl.ds(0, ig.shape[0]))]
+    for src, buf, dst in ((up, up_v, up_out), (dn, dn_v, dn_out)):
+        n = src.shape[0] // 4
+        steps += [(src, buf, dst, pl.ds(i * n, n)) for i in range(4)]
+    loads = [pltpu.make_async_copy(s.at[r], v.at[r], sem.at[0, i]) for i, (s, v, d, r) in enumerate(steps)]
+    stores = [pltpu.make_async_copy(v.at[r], d.at[r], sem.at[1, i]) for i, (s, v, d, r) in enumerate(steps)]
+    for copy in loads:
+        copy.start()
+    for load, store in zip(loads, stores):
+        load.wait()
+        store.start()
+    for copy in stores:
+        copy.wait()
 
 
 def per_device(H, inputs, out_grad, pre_act, w_up, w_down):
@@ -259,13 +375,14 @@
     vmem = pl.BlockSpec(memory_space=pltpu.VMEM)
     hbm = pl.BlockSpec(memory_space=pl.ANY)
     dma = pltpu.SemaphoreType.DMA
-    return pl.pallas_call(
+    shapes = (
+        jax.ShapeDtypeStruct((32, D), BF16),
+        jax.ShapeDtypeStruct((D, F), BF16),
+        jax.ShapeDtypeStruct((F, D), BF16),
+    )
+    results = pl.pallas_call(
         functools.partial(kernel, H),
-        out_shape=(
-            jax.ShapeDtypeStruct((32, D), BF16),
-            jax.ShapeDtypeStruct((D, F), BF16),
-            jax.ShapeDtypeStruct((F, D), BF16),
-        ),
+        out_shape=shapes,
         in_specs=[vmem, vmem, vmem, hbm, hbm],
         out_specs=(vmem, hbm, hbm),
         scratch_shapes=[
@@ -278,21 +395,27 @@
             pltpu.VMEM((COLS, 2, H, R, F), BF16),
             pltpu.VMEM((ROWS, 2, 2, H, R, F), BF16),
             pltpu.VMEM((COLS, 2, H, R, F), BF16),
-            pltpu.VMEM((H, COLS, R, D), BF16),
-            pltpu.VMEM((H, COLS, R, D), BF16),
-            pltpu.VMEM((COLS, R, D), F32),
-            pltpu.VMEM((H, COLS, R, D), BF16),
-            pltpu.VMEM((COLS, H, R, D), BF16),
+            pltpu.VMEM((H, 2, 8, 2, R, D), BF16),
+            pltpu.VMEM((H, 2, 8, R, D), BF16),
+            pltpu.VMEM((H, 2, 8, 2, R, D), F32),
+            pltpu.VMEM((H, 8, R, D), BF16),
+            pltpu.VMEM((H, 8, R, D), BF16),
+            pltpu.VMEM((H, 8, R, D), BF16),
+            pltpu.VMEM((H, R, D), F32),
+            pltpu.VMEM((8, H, R, D), BF16),
             pltpu.VMEM((D, F), BF16),
             pltpu.VMEM((F, D), BF16),
             dma((2,)),
-            dma((H, COLS)), dma((H, COLS)), dma((H,)), dma((H,)),
-            dma((COLS,)), dma((COLS,)), dma, dma,
+            dma((H,)), dma((H,)),
+            dma((H, 16)), dma((H, 16)), dma((H,)), dma((H,)),
+            dma, dma,
+            dma((16,)), dma((16,)), dma, dma,
             dma((ROWS,)), dma((ROWS,)),
             dma((H, 2, ROWS)), dma((H, 2, ROWS)),
             dma((H, ROWS)), dma((H, ROWS)),
-            dma((H,)), dma((H,)),
-            dma((H, COLS)), dma((H, COLS)),
+            dma((H, 2)), dma((H, 2)),
+            dma((H, 8)), dma((H, 8)),
+            dma((H, 8)), dma((H, 8)),
             dma((F // TILE + D // TILE,)),
         ],
         compiler_params=pltpu.CompilerParams(
@@ -300,6 +423,14 @@
         ),
         cost_estimate=pl.CostEstimate(flops=8 * 1024 * 1536 * 768, bytes_accessed=10 * 2**20, transcendentals=128 * 768),
     )(inputs, out_grad, pre_act, w_up, w_down)
+    return pl.pallas_call(
+        copy_kernel,
+        out_shape=shapes,
+        in_specs=[hbm] * 3,
+        out_specs=(hbm,) * 3,
+        scratch_shapes=[pltpu.VMEM(r.shape, BF16) for r in shapes] + [dma((2, 9))],
+        compiler_params=pltpu.CompilerParams(vmem_limit_bytes=56 * 2**20),
+    )(*results)
 
 
 def solution(mesh):

time: 143 us -> 101 us (0.71); the launches traced: 141 us -> 101 us
  Pallas kernels: 134 us -> 99.9 us
  local copies, waits for them, and re-layouts: 6.32 us -> 0 us
    pallas_call x1 -> x2, Pallas kernels: 134 us -> 99.9 us  [the longest x1 95.6 us: per_device(): pl.pallas_call(functools.partial(kernel, H), out_shape=shapes, in_specs=[...]
    unnamed x5 -> x0, local copies, waits for them, and re-layouts: 6.32 us -> none
where the time goes in v2:
time: 101 us
  Pallas kernels  99.9 us (99%)
    pallas_call x1, Pallas kernels, per_device(): pl.pallas_call(functools.partial(kernel, H), out_shape=shapes, in_specs=[...  95.6 us
    pallas_call x1, Pallas kernels, per_device(): pl.pallas_call(copy_kernel, out_shape=shapes, in_specs=[hbm] * 3, out_spe...  4.3 us

profile of v2, /device:TPU:1, one launch (start us, length us, event | category | flops | bytes accessed | tf_op | source)
XLA Modules:
  0.0 100.6 jit_solution(16043523074206301271)
XLA Ops:
  0.6 95.6 %shard_map.76 = (bf16[32,1536]{1,0:T(8,128)(2,1)}, bf16[1536,768]{1,0:T(8,128)(2,1)}, bf16[768,1536]{1,0:T(8,128)(2,1)}) custom-call(bf16[32,1536]{1,0:T(8,128)(2,1)} %in_ref.1, bf16[32,1536]{1,0:T(8,128)(2,1)} %og_ref.1, bf16[128,768]{1,0:T(8,128)(2,1)} %pre_ref.1, bf16[1536,768]{1,0:T(8,128)(2,1)} %wup_hbm.1, bf16[768,1536]{1,0:T(8,128)(2,1)} %wdn_hbm.1), custom_call_target="tpu_custom_call" | custom-call | flops 9663676416 | bytes 10485760 | tf_op jit(solution)/shard_map/pallas_call | solution.py:383
  96.3 4.3 %shard_map.77 = (bf16[32,1536]{1,0:T(8,128)(2,1)}, bf16[1536,768]{1,0:T(8,128)(2,1)}, bf16[768,1536]{1,0:T(8,128)(2,1)}) custom-call(bf16[32,1536]{1,0:T(8,128)(2,1)} %get-tuple-element.6.ig, bf16[1536,768]{1,0:T(8,128)(2,1)} %get-tuple-element.7.up, bf16[768,1536]{1,0:T(8,128)(2,1)} %get-tuple-element.8.dn), custom_call_target="tpu_custom_call" | custom-call | tf_op jit(solution)/shard_map/pallas_call | solution.py:426

commit v3 on v2

--- a/solution.py
+++ b/solution.py
@@ -21,8 +21,8 @@
     H,
     in_ref, og_ref, pre_ref, wup_hbm, wdn_hbm,
     ig_out, up_hbm, dn_hbm,
-    wup, wdn, slope, grads, ins, acts, part, rsr, hid, igs, igr, igf, igb, igx, igz, igo, fin, up, dn,
-    wsem, gxs, gxr, gs, gr, gfs, gfr, xxs, xxr, xs, xr, xfs, xfr, as_, ar, ps, pr, hs, hr, ss, sr,
+    wup, wdn, slope, grads, ins, acts, part, prx, p2s, p2r, q1r, q2s, q2r, hid, igs, igr, igf, igb, igx, igz, igo, fin, up, dn,
+    wsem, gxs, gxr, gs, gr, gfs, gfr, xxs, xxr, xs, xr, xfs, xfr, as_, ar, pxs, pxr, p2ss, p2rs, q1ss, q1rs, q2ss, q2rs, hs, hr, hxs, hxr, ss, sr,
     bxs, bxr, is_, ir, osem,
 ):
     R = 32 // H
@@ -50,6 +50,13 @@
     def row_dev(o):
         return (row_at(o), col)
 
+    def y_at(dy):
+        return lax.rem(y + dy, 4)
+
+    def y_dev(dy):
+        return (y_at(dy) * 2 + xh, col)
+
+    across = (y * 2 + 1 - xh, col)
     sib = (row, chip * 2 + 1 - k)
 
     def each(lo, hi, f):
@@ -75,27 +82,37 @@
     pl.semaphore_signal(barrier, inc=1, device_id=sib, device_id_type=MESH)
     pl.semaphore_wait(barrier, 7 + 1 + 1 + ROWS - 1)
 
-    def ring_block(p, d, s):
-        return (xl * 8 if p == 0 else other) + z_at((9 - s) % 8 if d == 0 else s - 1)
+    RING = {1: (0, 1), 2: (1, 1), 3: (2, 1), 4: (3, 1)}
+    FAST = {1: (0, 1), 2: (0, 2), 3: (2, 1), 4: (2, 2)}
+
+    def ring_block(way, p, d, s):
+        back = way[s][0]
+        return (xl * 8 if p == 0 else other) + z_at((8 - back) % 8 if d == 0 else back)
+
+    def ring_dev(way, d, s):
+        return z_dev(way[s][1] if d == 0 else 8 - way[s][1])
 
     def ring_ok(p, d, s):
         return s < 4 or (s == 4 and p == d)
 
+    def grad_way(h):
+        return FAST if H == 2 and h == 0 else RING
+
     def c_gradx(h):
         return remote(grads.at[chip, k, h], grads.at[chip, k, h], gxs.at[h], gxr.at[h], partner)
 
     def c_grad(h, p, d, s):
-        block = grads.at[ring_block(p, d, s), k, h]
+        block = grads.at[ring_block(grad_way(h), p, d, s), k, h]
         i = (p * 2 + d) * 4 + s - 1
-        return remote(block, block, gs.at[h, i], gr.at[h, i], z_dev(1 if d == 0 else 7))
+        return remote(block, block, gs.at[h, i], gr.at[h, i], ring_dev(grad_way(h), d, s))
 
     def c_inx():
         return remote(ins.at[chip, k], ins.at[chip, k], xxs, xxr, partner)
 
     def c_in(p, d, s):
-        block = ins.at[ring_block(p, d, s), k]
+        block = ins.at[ring_block(RING, p, d, s), k]
         i = (p * 2 + d) * 4 + s - 1
-        return remote(block, block, xs.at[i], xr.at[i], z_dev(1 if d == 0 else 7))
+        return remote(block, block, xs.at[i], xr.at[i], ring_dev(RING, d, s))
 
     def c_gradf(h):
         return remote(grads.at[:, k, h], grads.at[:, k, h], gfs.at[h], gfr.at[h], sib)
@@ -106,15 +123,30 @@
     def c_act(o):
         return remote(acts.at[pl.ds(2 * row, 2)], acts.at[pl.ds(2 * row, 2)], as_.at[o], ar.at[o], row_dev(o))
 
-    def c_part(h, q, o):
-        kk = k if q == 0 else 1 - k
-        return remote(
-            part.at[pl.ds(2 * row_at(o), 2), kk, h], rsr.at[o, :, kk, h], ps.at[h, q, o], pr.at[h, q, o], row_dev(o)
-        )
-
-    def c_hid(h, o):
-        block = hid.at[pl.ds(2 * row, 2), :, h]
-        return remote(block, block, hs.at[h, o], hr.at[h, o], row_dev(o))
+    def c_px(h):
+        return remote(part.at[:, 1 - xh, :, k, h], prx.at[h], pxs.at[h], pxr.at[h], across)
+
+    def c_p2(h, dy):
+        return remote(p2s.at[h, dy], p2r.at[h, dy], p2ss.at[h, dy], p2rs.at[h, dy], y_dev(dy))
+
+    def c_q1(h, dy):
+        return remote(part.at[y_at(dy), :, :, 1 - k, h], q1r.at[h, dy], q1ss.at[h, dy], q1rs.at[h, dy], y_dev(dy))
+
+    def c_q2(h):
+        return remote(q2s.at[h], q2r.at[h], q2ss.at[h], q2rs.at[h], across)
+
+    def c_hid(h, i, dy):
+        if i == 0:
+            block, dev = hid.at[y, xh, :, :, h], y_dev(dy)
+        elif i == 1:
+            block, dev = hid.at[y, 1 - xh, :, 0, h], y_dev(dy)
+        else:
+            block, dev = hid.at[y_at(4 - dy), xh, :, 1, h], across
+        return remote(block, block, hs.at[h, i, dy], hr.at[h, i, dy], dev)
+
+    def c_hidx(h):
+        block = hid.at[y, xh, :, :, h]
+        return remote(block, block, hxs.at[h], hxr.at[h], across)
 
     def c_igs(h, c):
         return remote(igs.at[h, c, :, 1 - k], igr.at[h, c], ss.at[h, c], sr.at[h, c], sib)
@@ -125,11 +157,15 @@
     def c_ig(h, o):
         return remote(igz.at[h, z_at(o)], fin.at[o, h], is_.at[h, o], ir.at[h, o], z_dev(o))
 
+    def grad_first(h, p):
+        for s in (1, 2) if grad_way(h) is FAST else (1,):
+            for d in range(2):
+                c_grad(h, p, d, s).start()
+
     for h in range(H):
         grads[chip, k, h] = og_ref[h * R:(h + 1) * R]
-        for d in range(2):
-            c_grad(h, 0, d, 1).start()
         c_gradx(h).start()
+        grad_first(h, 0)
     ins[chip, k] = in_ref[...]
 
     def gelu(b):
@@ -151,13 +187,9 @@
             cols = pl.ds(pl.multiple_of(n * TILE, TILE), TILE)
             lhs = grads[:, kk, h].reshape(16 * R, D)
             acc = lax.dot_general(lhs, wdn[cols, :], NT, preferred_element_type=F32)
-            part[:, kk, h, :, cols] = acc.astype(BF16).reshape(16, R, TILE)
+            part[:, :, :, kk, h, :, cols] = acc.astype(BF16).reshape(4, 2, 2, R, TILE)
         each(0, F // TILE, tile)
 
-    for h in range(H):
-        c_gradx(h).wait_recv()
-        for d in range(2):
-            c_grad(h, 1, d, 1).start()
     def grad_step(h, s):
         for p in range(2):
             for d in range(2):
@@ -166,24 +198,76 @@
                     if ring_ok(p, d, s + 1):
                         c_grad(h, p, d, s + 1).start()
 
-    for s in range(1, 4):
-        for h in range(H):
-            grad_step(h, s)
-
-    for h in range(H):
-        grad_step(h, 4)
+    def mm1_own(h):
         c_gradf(h).start()
-        if h == H - 1:
-            c_inx().start()
-            for d in range(2):
-                c_in(0, d, 1).start()
         if h == 0:
             wdn_copy.wait()
         mm1(h, k)
-        each(1, ROWS, lambda o: c_part(h, 0, o).start())
+        c_px(h).start()
+
+    def mm1_sib(h):
         c_gradf(h).wait_recv()
         mm1(h, 1 - k)
-        each(1, ROWS, lambda o: c_part(h, 1, o).start())
+        each(1, 4, lambda dy: c_q1(h, dy).start())
+
+    def add_p(h):
+        c_px(h).wait_recv()
+
+        def one(dy):
+            yy = y_at(dy)
+            p2s[h, dy] = (part[yy, xh, :, k, h].astype(F32) + prx[h, yy].astype(F32)).astype(BF16)
+            c_p2(h, dy).start()
+
+        each(1, 4, one)
+
+    def add_q(h):
+        each(1, 4, lambda dy: c_q1(h, dy).wait_recv())
+        acc = part[y, 1 - xh, :, 1 - k, h].astype(F32)
+        for dy in range(1, 4):
+            acc += q1r[h, dy, 1 - xh].astype(F32)
+        q2s[h] = acc.astype(BF16)
+        c_q2(h).start()
+
+    def in_first():
+        c_inx().start()
+        for d in range(2):
+            c_in(0, d, 1).start()
+
+    for h in range(H):
+        c_gradx(h).wait_recv()
+        grad_first(h, 1)
+    if H == 1:
+        for s in range(1, 5):
+            grad_step(0, s)
+        in_first()
+        mm1_own(0)
+        mm1_sib(0)
+        add_p(0)
+        add_q(0)
+    else:
+        for p in range(2):
+            for d in range(2):
+                c_grad(0, p, d, 2).wait_recv()
+                for s in (3, 4):
+                    if ring_ok(p, d, s):
+                        c_grad(0, p, d, s).start()
+        grad_step(1, 1)
+        for s in (1, 3, 4):
+            for p in range(2):
+                for d in range(2):
+                    if ring_ok(p, d, s):
+                        c_grad(0, p, d, s).wait_recv()
+        grad_step(1, 2)
+        mm1_own(0)
+        grad_step(1, 3)
+        mm1_sib(0)
+        grad_step(1, 4)
+        mm1_own(1)
+        in_first()
+        add_p(0)
+        mm1_sib(1)
+        add_q(0)
+        add_p(1)
 
     def in_step(s):
         for p in range(2):
@@ -211,47 +295,61 @@
         c_dn(m).start()
 
     def hidden(h):
-        each(1, ROWS, lambda o: c_part(h, 0, o).wait_recv())
-        each(1, ROWS, lambda o: c_part(h, 1, o).wait_recv())
-
-        def block(b):
-            zz, kk = lax.div(b, 2), lax.rem(b, 2)
-            acc = part[2 * row + zz, kk, h].astype(F32)
-            for o in range(1, ROWS):
-                acc += rsr[o, zz, kk, h].astype(F32)
-            hid[2 * row + zz, kk, h] = (acc * slope[zz, kk, h]).astype(BF16)
-
-        each(0, 4, block)
-        each(1, ROWS, lambda o: c_hid(h, o).start())
+        each(1, 4, lambda dy: c_p2(h, dy).wait_recv())
+        c_q2(h).wait_recv()
+
+        def block(zz):
+            acc = part[y, xh, zz, k, h].astype(F32) + prx[h, y, zz].astype(F32)
+            for dy in range(1, 4):
+                acc += p2r[h, dy, zz].astype(F32)
+            hid[y, xh, zz, k, h] = (acc * slope[zz, k, h]).astype(BF16)
+            acc = part[y, xh, zz, 1 - k, h].astype(F32) + q2r[h, zz].astype(F32)
+            for dy in range(1, 4):
+                acc += q1r[h, dy, xh, zz].astype(F32)
+            hid[y, xh, zz, 1 - k, h] = (acc * slope[zz, 1 - k, h]).astype(BF16)
+
+        each(0, 2, block)
+        c_hidx(h).start()
+        each(1, 4, lambda dy: c_hid(h, 0, dy).start())
+
+    def relay(h):
+        c_hidx(h).wait_recv()
+        each(1, 4, lambda dy: c_hid(h, 1, dy).start())
+
+        def one(dy):
+            c_hid(h, 0, dy).wait_recv()
+            c_hid(h, 2, dy).start()
+
+        each(1, 4, one)
 
     each(1, ROWS, lambda o: c_act(o).wait_recv())
     c_inx().wait_recv()
     for d in range(2):
         c_in(1, d, 1).start()
     if H == 1:
+        hidden(0)
         in_step(1)
         mm_dn(0)
-        hidden(0)
+        relay(0)
         in_step(2)
         mm_dn(1)
-        in_step(3)
         mm_dn(2)
-        in_step(4)
     else:
+        hidden(0)
+        add_q(1)
+        mm_dn(0)
         in_step(1)
-        hidden(0)
-        mm_dn(0)
+        hidden(1)
+        relay(0)
+        mm_dn(1)
         in_step(2)
-        hidden(1)
-        mm_dn(1)
-        in_step(3)
-        mm_dn(2)
+        relay(1)
 
     def mm_ig(h, c):
-        first = other if c == 0 else xl * 8
+        first = 2 * (1 - xl) if c == 0 else 2 * xl
         def tile(n):
             cols = pl.ds(pl.multiple_of(n * TILE, TILE), TILE)
-            lhs = hid[pl.ds(first, 8), :, h].reshape(16 * R, F)
+            lhs = hid[pl.ds(first, 2), :, :, :, h].reshape(16 * R, F)
             acc = lax.dot_general(lhs, wup[cols, :], NT, preferred_element_type=F32).reshape(8, 2, R, TILE)
             igf[h, c, :, :, :, cols] = acc
             igs[h, c, :, :, :, cols] = acc.astype(BF16)
@@ -275,7 +373,8 @@
     order = (4, 3, 5, 2, 6, 1, 7, 0)
 
     def ig(h):
-        each(1, ROWS, lambda o: c_hid(h, o).wait_recv())
+        each(1, 4, lambda dy: c_hid(h, 1, dy).wait_recv())
+        each(1, 4, lambda dy: c_hid(h, 2, dy).wait_recv())
         mm_ig(h, 0)
         c_igs(h, 0).start()
         mm_ig(h, 1)
@@ -283,24 +382,23 @@
         c_igs(h, 0).wait_recv()
         for o in order:
             share(h, o)
-        if h == 0:
-            if H == 2:
-                in_step(4)
-            c_inf().start()
-        c_igs(h, 1).wait_recv()
 
     wup_copy.wait()
     ig(0)
+    in_step(3)
     if H == 2:
-        for o in order[:4]:
+        ig(1)
+        c_igs(0, 1).wait_recv()
+        for i, o in enumerate(order):
             pass_on(0, o)
-        ig(1)
-        for o in order[4:]:
-            pass_on(0, o)
-    for o in order:
-        pass_on(H - 1, o)
-
-    c_inf().wait_recv()
+            if i == 3:
+                in_step(4)
+                c_inf().start()
+        mm_dn(2)
+    else:
+        in_step(4)
+        c_inf().start()
+    c_igs(H - 1, 1).wait_recv()
 
     def c_up(m):
         rows = pl.ds(m * TILE, TILE)
@@ -314,7 +412,12 @@
         up[pl.ds(m * TILE, TILE), :] = (acc * scale).astype(BF16)
         c_up(m).start()
 
-    each(0, D // TILE, mm_up)
+    for i, o in enumerate(order):
+        pass_on(H - 1, o)
+        if i == 0:
+            c_inf().wait_recv()
+        if i < D // TILE:
+            mm_up(i)
 
     for h in range(H):
         each(1, 8, lambda o: c_ig(h, o).wait_recv())
@@ -338,9 +441,13 @@
     for h in range(H):
         c_gradx(h).wait_send()
         c_gradf(h).wait_send()
-        for q in range(2):
-            each(1, ROWS, lambda o: c_part(h, q, o).wait_send())
-        each(1, ROWS, lambda o: c_hid(h, o).wait_send())
+        c_px(h).wait_send()
+        each(1, 4, lambda dy: c_p2(h, dy).wait_send())
+        each(1, 4, lambda dy: c_q1(h, dy).wait_send())
+        c_q2(h).wait_send()
+        c_hidx(h).wait_send()
+        for i in range(3):
+            each(1, 4, lambda dy: c_hid(h, i, dy).wait_send())
         for c in range(2):
             c_igs(h, c).wait_send()
         each(0, 8, lambda o: c_igx(h, o).wait_send())
@@ -392,9 +499,14 @@
             pltpu.VMEM((COLS, 2, H, R, D), BF16),
             pltpu.VMEM((COLS, 2, 32, D), BF16),
             pltpu.VMEM((COLS, 2, 32, F), BF16),
-            pltpu.VMEM((COLS, 2, H, R, F), BF16),
-            pltpu.VMEM((ROWS, 2, 2, H, R, F), BF16),
-            pltpu.VMEM((COLS, 2, H, R, F), BF16),
+            pltpu.VMEM((4, 2, 2, 2, H, R, F), BF16),
+            pltpu.VMEM((H, 4, 2, R, F), BF16),
+            pltpu.VMEM((H, 4, 2, R, F), BF16),
+            pltpu.VMEM((H, 4, 2, R, F), BF16),
+            pltpu.VMEM((H, 4, 2, 2, R, F), BF16),
+            pltpu.VMEM((H, 2, R, F), BF16),
+            pltpu.VMEM((H, 2, R, F), BF16),
+            pltpu.VMEM((4, 2, 2, 2, H, R, F), BF16),
             pltpu.VMEM((H, 2, 8, 2, R, D), BF16),
             pltpu.VMEM((H, 2, 8, R, D), BF16),
             pltpu.VMEM((H, 2, 8, 2, R, D), F32),
@@ -411,8 +523,12 @@
             dma, dma,
             dma((16,)), dma((16,)), dma, dma,
             dma((ROWS,)), dma((ROWS,)),
-            dma((H, 2, ROWS)), dma((H, 2, ROWS)),
-            dma((H, ROWS)), dma((H, ROWS)),
+            dma((H,)), dma((H,)),
+            dma((H, 4)), dma((H, 4)),
+            dma((H, 4)), dma((H, 4)),
+            dma((H,)), dma((H,)),
+            dma((H, 3, 4)), dma((H, 3, 4)),
+            dma((H,)), dma((H,)),
             dma((H, 2)), dma((H, 2)),
             dma((H, 8)), dma((H, 8)),
             dma((H, 8)), dma((H, 8)),

time: 101 us -> 95.6 us (0.947)
  Pallas kernels: 99.9 us -> 94.8 us
    pallas_call x1, Pallas kernels: 95.6 us -> 90.5 us  [per_device(): pl.pallas_call(functools.partial(kernel, H), out_shape=shapes, in_specs=[...]
where the time goes in v3:
time: 95.6 us; the launch traced here: 95.5 us
  Pallas kernels  94.8 us (99%)
    pallas_call x1, Pallas kernels, per_device(): pl.pallas_call(functools.partial(kernel, H), out_shape=shapes, in_specs=[...  90.5 us
    pallas_call x1, Pallas kernels, per_device(): pl.pallas_call(copy_kernel, out_shape=shapes, in_specs=[hbm] * 3, out_spe...  4.3 us

profile of v3, /device:TPU:1, one launch (start us, length us, event | category | flops | bytes accessed | tf_op | source)
XLA Modules:
  0.0 95.5 jit_solution(3506392983168369433)
XLA Ops:
  0.6 90.5 %shard_map.76 = (bf16[32,1536]{1,0:T(8,128)(2,1)}, bf16[1536,768]{1,0:T(8,128)(2,1)}, bf16[768,1536]{1,0:T(8,128)(2,1)}) custom-call(bf16[32,1536]{1,0:T(8,128)(2,1)} %in_ref.1, bf16[32,1536]{1,0:T(8,128)(2,1)} %og_ref.1, bf16[128,768]{1,0:T(8,128)(2,1)} %pre_ref.1, bf16[1536,768]{1,0:T(8,128)(2,1)} %wup_hbm.1, bf16[768,1536]{1,0:T(8,128)(2,1)} %wdn_hbm.1), custom_call_target="tpu_custom_call" | custom-call | flops 9663676416 | bytes 10485760 | tf_op jit(solution)/shard_map/pallas_call | solution.py:490
  91.2 4.3 %shard_map.77 = (bf16[32,1536]{1,0:T(8,128)(2,1)}, bf16[1536,768]{1,0:T(8,128)(2,1)}, bf16[768,1536]{1,0:T(8,128)(2,1)}) custom-call(bf16[32,1536]{1,0:T(8,128)(2,1)} %get-tuple-element.6.ig, bf16[1536,768]{1,0:T(8,128)(2,1)} %get-tuple-element.7.up, bf16[768,1536]{1,0:T(8,128)(2,1)} %get-tuple-element.8.dn), custom_call_target="tpu_custom_call" | custom-call | tf_op jit(solution)/shard_map/pallas_call | solution.py:542

commit v4 on v3

--- a/solution.py
+++ b/solution.py
@@ -22,8 +22,8 @@
     in_ref, og_ref, pre_ref, wup_hbm, wdn_hbm,
     ig_out, up_hbm, dn_hbm,
     wup, wdn, slope, grads, ins, acts, part, prx, p2s, p2r, q1r, q2s, q2r, hid, igs, igr, igf, igb, igx, igz, igo, fin, up, dn,
-    wsem, gxs, gxr, gs, gr, gfs, gfr, xxs, xxr, xs, xr, xfs, xfr, as_, ar, pxs, pxr, p2ss, p2rs, q1ss, q1rs, q2ss, q2rs, hs, hr, hxs, hxr, ss, sr,
-    bxs, bxr, is_, ir, osem,
+    wsem, gys, gyr, gxs, gxr, gs, gr, gfs, gfr, xxs, xxr, xs, xr, xfs, xfr, as_, ar, pxs, pxr, p2ss, p2rs, q1ss, q1rs, q2ss, q2rs, hs, hr, hxs, hxr, ss, sr,
+    bxs, bxr, is_, ir, axs, axr, osem,
 ):
     R = 32 // H
     D = in_ref.shape[1]
@@ -96,7 +96,7 @@
         return s < 4 or (s == 4 and p == d)
 
     def grad_way(h):
-        return FAST if H == 2 and h == 0 else RING
+        return RING
 
     def c_gradx(h):
         return remote(grads.at[chip, k, h], grads.at[chip, k, h], gxs.at[h], gxr.at[h], partner)
@@ -106,6 +106,10 @@
         i = (p * 2 + d) * 4 + s - 1
         return remote(block, block, gs.at[h, i], gr.at[h, i], ring_dev(grad_way(h), d, s))
 
+    def c_gx(d, s):
+        block = grads.at[xl * 8 + z_at(8 - s if d == 0 else s), k, 1]
+        return remote(block, block, gys.at[d * 4 + s - 1], gyr.at[d * 4 + s - 1], partner)
+
     def c_inx():
         return remote(ins.at[chip, k], ins.at[chip, k], xxs, xxr, partner)
 
@@ -120,8 +124,14 @@
     def c_inf():
         return remote(ins.at[:, k], ins.at[:, k], xfs, xfr, sib)
 
-    def c_act(o):
-        return remote(acts.at[pl.ds(2 * row, 2)], acts.at[pl.ds(2 * row, 2)], as_.at[o], ar.at[o], row_dev(o))
+    def c_actx():
+        block = acts.at[pl.ds(2 * row, 2)]
+        return remote(block, block, axs, axr, across)
+
+    def c_act(p, dy):
+        r = y * 2 + (xh if p == 0 else 1 - xh)
+        block = acts.at[pl.ds(2 * r, 2)]
+        return remote(block, block, as_.at[p, dy], ar.at[p, dy], y_dev(dy))
 
     def c_px(h):
         return remote(part.at[:, 1 - xh, :, k, h], prx.at[h], pxs.at[h], pxr.at[h], across)
@@ -180,7 +190,8 @@
             slope[lax.div(b, 2), lax.rem(b, 2), h] = sl[h * R:(h + 1) * R]
 
     each(0, 4, gelu)
-    each(1, ROWS, lambda o: c_act(o).start())
+    c_actx().start()
+    each(1, 4, lambda dy: c_act(0, dy).start())
 
     def mm1(h, kk):
         def tile(n):
@@ -198,6 +209,14 @@
                     if ring_ok(p, d, s + 1):
                         c_grad(h, p, d, s + 1).start()
 
+    def b_step(s):
+        for d in range(2):
+            if ring_ok(0, d, s):
+                c_grad(1, 0, d, s).wait_recv()
+                if ring_ok(0, d, s + 1):
+                    c_grad(1, 0, d, s + 1).start()
+                c_gx(d, s).start()
+
     def mm1_own(h):
         c_gradf(h).start()
         if h == 0:
@@ -233,9 +252,10 @@
         for d in range(2):
             c_in(0, d, 1).start()
 
-    for h in range(H):
-        c_gradx(h).wait_recv()
-        grad_first(h, 1)
+    c_gradx(0).wait_recv()
+    grad_first(0, 1)
+    c_actx().wait_recv()
+    each(1, 4, lambda dy: c_act(1, dy).start())
     if H == 1:
         for s in range(1, 5):
             grad_step(0, s)
@@ -245,23 +265,21 @@
         add_p(0)
         add_q(0)
     else:
-        for p in range(2):
+        grad_step(0, 1)
+        b_step(1)
+        grad_step(0, 2)
+        b_step(2)
+        grad_step(0, 3)
+        b_step(3)
+        grad_step(0, 4)
+        mm1_own(0)
+        mm1_sib(0)
+        b_step(4)
+        c_gradx(1).wait_recv()
+        for s in range(1, 5):
             for d in range(2):
-                c_grad(0, p, d, 2).wait_recv()
-                for s in (3, 4):
-                    if ring_ok(p, d, s):
-                        c_grad(0, p, d, s).start()
-        grad_step(1, 1)
-        for s in (1, 3, 4):
-            for p in range(2):
-                for d in range(2):
-                    if ring_ok(p, d, s):
-                        c_grad(0, p, d, s).wait_recv()
-        grad_step(1, 2)
-        mm1_own(0)
-        grad_step(1, 3)
-        mm1_sib(0)
-        grad_step(1, 4)
+                if ring_ok(0, d, s):
+                    c_gx(d, s).wait_recv()
         mm1_own(1)
         in_first()
         add_p(0)
@@ -322,7 +340,8 @@
 
         each(1, 4, one)
 
-    each(1, ROWS, lambda o: c_act(o).wait_recv())
+    for p in range(2):
+        each(1, 4, lambda dy: c_act(p, dy).wait_recv())
     c_inx().wait_recv()
     for d in range(2):
         c_in(1, d, 1).start()
@@ -435,8 +454,10 @@
         for d in range(2):
             for t in range(1, 5):
                 if ring_ok(p, d, t):
-                    for h in range(H):
-                        c_grad(h, p, d, t).wait_send()
+                    c_grad(0, p, d, t).wait_send()
+                    if H == 2 and p == 0:
+                        c_grad(1, 0, d, t).wait_send()
+                        c_gx(d, t).wait_send()
                     c_in(p, d, t).wait_send()
     for h in range(H):
         c_gradx(h).wait_send()
@@ -454,7 +475,9 @@
         each(1, 8, lambda o: c_ig(h, o).wait_send())
     c_inx().wait_send()
     c_inf().wait_send()
-    each(1, ROWS, lambda o: c_act(o).wait_send())
+    c_actx().wait_send()
+    for p in range(2):
+        each(1, 4, lambda dy: c_act(p, dy).wait_send())
     each(0, F // TILE, lambda m: c_dn(m).wait())
     each(0, D // TILE, lambda m: c_up(m).wait())
 
@@ -518,11 +541,12 @@
             pltpu.VMEM((D, F), BF16),
             pltpu.VMEM((F, D), BF16),
             dma((2,)),
+            dma((8,)), dma((8,)),
             dma((H,)), dma((H,)),
             dma((H, 16)), dma((H, 16)), dma((H,)), dma((H,)),
             dma, dma,
             dma((16,)), dma((16,)), dma, dma,
-            dma((ROWS,)), dma((ROWS,)),
+            dma((2, 4)), dma((2, 4)),
             dma((H,)), dma((H,)),
             dma((H, 4)), dma((H, 4)),
             dma((H, 4)), dma((H, 4)),
@@ -532,6 +556,7 @@
             dma((H, 2)), dma((H, 2)),
             dma((H, 8)), dma((H, 8)),
             dma((H, 8)), dma((H, 8)),
+            dma, dma,
             dma((F // TILE + D // TILE,)),
         ],
         compiler_params=pltpu.CompilerParams(

time: 95.6 us -> 99.3 us (1.039)
  Pallas kernels: 94.8 us -> 98.5 us
    pallas_call x1, Pallas kernels: 90.5 us -> 94.2 us  [per_device(): pl.pallas_call(functools.partial(kernel, H), out_shape=shapes, in_specs=[...]
where the time goes in v4:
time: 99.3 us; the launch traced here: 99.2 us
  Pallas kernels  98.5 us (99%)
    pallas_call x1, Pallas kernels, per_device(): pl.pallas_call(functools.partial(kernel, H), out_shape=shapes, in_specs=[...  94.2 us
    pallas_call x1, Pallas kernels, per_device(): pl.pallas_call(copy_kernel, out_shape=shapes, in_specs=[hbm] * 3, out_spe...  4.3 us

profile of v4, /device:TPU:1, one launch (start us, length us, event | category | flops | bytes accessed | tf_op | source)
XLA Modules:
  0.0 99.2 jit_solution(13128328858392792729)
XLA Ops:
  0.6 94.2 %shard_map.76 = (bf16[32,1536]{1,0:T(8,128)(2,1)}, bf16[1536,768]{1,0:T(8,128)(2,1)}, bf16[768,1536]{1,0:T(8,128)(2,1)}) custom-call(bf16[32,1536]{1,0:T(8,128)(2,1)} %in_ref.1, bf16[32,1536]{1,0:T(8,128)(2,1)} %og_ref.1, bf16[128,768]{1,0:T(8,128)(2,1)} %pre_ref.1, bf16[1536,768]{1,0:T(8,128)(2,1)} %wup_hbm.1, bf16[768,1536]{1,0:T(8,128)(2,1)} %wdn_hbm.1), custom_call_target="tpu_custom_call" | custom-call | flops 9663676416 | bytes 10485760 | tf_op jit(solution)/shard_map/pallas_call | solution.py:513
  94.8 4.3 %shard_map.77 = (bf16[32,1536]{1,0:T(8,128)(2,1)}, bf16[1536,768]{1,0:T(8,128)(2,1)}, bf16[768,1536]{1,0:T(8,128)(2,1)}) custom-call(bf16[32,1536]{1,0:T(8,128)(2,1)} %get-tuple-element.6.ig, bf16[1536,768]{1,0:T(8,128)(2,1)} %get-tuple-element.7.up, bf16[768,1536]{1,0:T(8,128)(2,1)} %get-tuple-element.8.dn), custom_call_target="tpu_custom_call" | custom-call | tf_op jit(solution)/shard_map/pallas_call | solution.py:567
